TPU v7x, 128 devices: a whole 4x4x4 slice. The times are simulated.
128 devices in a mesh: dp: 64 (over y_hi, x, z, core), tensor: 2 (over y_lo).
Axes of the slice: x: 4, y: 4 (y_hi: 2, y_lo: 2; y = y_hi * 2 + y_lo), z: 4, core: 2. Of those that a mesh axis runs over, the one named last changes fastest.
Arguments:
- queries: bfloat16 [2, 64, 256, 4096], P(None, 'dp', None, 'tensor'), may hold values from -160 to 160
- trace_kv: bfloat16 [2, 64, 256, 2, 512], P(None, 'dp', None, None, 'tensor'), may hold values from -4 to 4
- lengths: int32 [2, 64], P(None, 'dp'), may hold values from 32 to 256, as said below
- prompt_kv: bfloat16 [1024, 2, 512], P(('dp', 'tensor')), may hold values from -4 to 4
Outputs:
- attended: bfloat16 [2, 64, 256, 4096], P(None, 'dp', None, 'tensor')
Inputs may be any that keep to these rules, and one draw needn't show every extreme that they name: lengths do not rise with rank (row-major order of the array); the first is 256 and the last is 32.
All inputs are finite; a program needn't handle non-finite values.
Results may differ from a plain program's by a relative error of at most 0.0045.
Values may be sent and summed in bfloat16 or wider, within the bound.
A program may use at most 64 MiB of HBM per device.

v0:
```python
import jax
import jax.numpy as jnp
from jax import lax
from jax.sharding import PartitionSpec as P

HEAD = 128


def attend_block(query_rows, prompt_cols, own_cols, start, length):
    groups = prompt_cols.shape[-1] // HEAD
    rows = query_rows.shape[0]
    per_group = query_rows.shape[1] // (groups * HEAD)
    score_scale = 1.0 / jnp.sqrt(jnp.float32(HEAD))
    query_heads = query_rows.reshape(rows, groups, per_group, HEAD)
    prompt_keys = prompt_cols[:, 0].reshape(prompt_cols.shape[0], groups, HEAD)
    prompt_values = prompt_cols[:, 1].reshape(prompt_cols.shape[0], groups, HEAD)
    own_count = own_cols.shape[0]
    own_keys = own_cols[:, 0].reshape(own_count, groups, HEAD)
    own_values = own_cols[:, 1].reshape(own_count, groups, HEAD)
    prompt_scores = (
        jnp.einsum("tgqd,sgd->gqts", query_heads, prompt_keys, preferred_element_type=jnp.float32)
        * score_scale
    )
    own_scores = (
        jnp.einsum("tgqd,sgd->gqts", query_heads, own_keys, preferred_element_type=jnp.float32)
        * score_scale
    )
    token_pos = start + jnp.arange(rows, dtype=jnp.int32)
    key_pos = jnp.arange(own_count, dtype=jnp.int32)
    allowed = (key_pos[None, :] <= token_pos[:, None]) & (key_pos[None, :] < length)
    own_scores = jnp.where(allowed, own_scores, -1e30)
    top = jnp.maximum(jnp.max(prompt_scores, axis=-1), jnp.max(own_scores, axis=-1))
    prompt_weights = jnp.exp(prompt_scores - top[..., None])
    own_weights = jnp.where(allowed, jnp.exp(own_scores - top[..., None]), 0.0)
    totals = jnp.sum(prompt_weights, axis=-1) + jnp.sum(own_weights, axis=-1)
    summed = jnp.einsum(
        "gqts,sgd->gqtd",
        prompt_weights.astype(jnp.bfloat16),
        prompt_values,
        preferred_element_type=jnp.float32,
    )
    summed = summed + jnp.einsum(
        "gqts,sgd->gqtd",
        own_weights.astype(jnp.bfloat16),
        own_values,
        preferred_element_type=jnp.float32,
    )
    result = summed / totals[..., None]
    result = jnp.transpose(result, (2, 0, 1, 3)).reshape(rows, -1)
    result = jnp.where(token_pos[:, None] < length, result, 0.0)
    return result.astype(jnp.bfloat16)


def attend_slot(query_rows, kv_rows, length, prompt_cols):
    tokens = query_rows.shape[0]
    blocks = 4
    block_rows = tokens // blocks
    pieces = []
    for block in range(blocks):
        start = block * block_rows
        end = start + block_rows
        block_queries = query_rows[start:end]
        own_cols = kv_rows[:end]

        def compute(operands):
            return attend_block(operands[0], operands[1], operands[2], start, length)

        def skip(operands):
            return jnp.zeros((block_rows, query_rows.shape[1]), jnp.bfloat16)

        pieces.append(
            lax.cond(start < length, compute, skip, (block_queries, prompt_cols, own_cols))
        )
    return jnp.concatenate(pieces, axis=0)


def per_device(queries, trace_kv, lengths, prompt_kv):
    slot_queries = queries[:, 0]
    slot_kv = trace_kv[:, 0]
    slot_lengths = lengths[:, 0]
    columns_dev = slot_kv.shape[-1]
    whole_prompt = lax.all_gather(prompt_kv, ("dp", "tensor"), axis=0, tiled=True)
    prompt_cols = lax.dynamic_slice_in_dim(
        whole_prompt, lax.axis_index("tensor") * columns_dev, columns_dev, 2
    )
    first_out = attend_slot(slot_queries[0], slot_kv[0], slot_lengths[0], prompt_cols)
    second_out = attend_slot(slot_queries[1], slot_kv[1], slot_lengths[1], prompt_cols)
    return jnp.stack([first_out, second_out])[:, None]


def solution(mesh):
    placed = (
        P(None, "dp", None, "tensor"),
        P(None, "dp", None, None, "tensor"),
        P(None, "dp"),
        P(("dp", "tensor"), None, None),
    )
    return jax.shard_map(
        per_device,
        mesh=mesh,
        in_specs=placed,
        out_specs=P(None, "dp", None, "tensor"),
        check_vma=False,
    )
```

profile of v0, /device:TPU:1, one launch (start us, length us, event | category | flops | bytes accessed | tf_op | source)
XLA Modules:
  0.0 416.3 jit_solution(17292737636384897044)
XLA Ops:
  7.3 1.4 fusion.288
  13.9 299.9 %all-gather.2.cloned.1.call-done = bf16[1024,2,512]{2,1,0:T(2,128)(2,1)} async-done(((bf16[8,2,512]{2,1,0:T(2,128)(2,1)}), bf16[1024,2,512]{2,1,0:T(2,128)(2,1)}) %all-gather.2.cloned.1.call-update) | async-done | bytes 2097168 | tf_op jit(solution)/shard_map/all_gather | solution.py:82
  313.8 1.9 constant_dynamic-slice_fusion
  315.7 10.1 %conditional.11 = (bf16[64,2048]{1,0:T(8,128)(2,1)S(1)}) conditional(s32[]{:T(128)} %convert_element_type.99, () %tuple.57, (s32[]{:T(128)}, bf16[1024,2,256]{2,1,0:T(2,128)(2,1)S(1)}, bf16[2,1,256,2048]{3,2,1,0:T(8,128)(2,1)}, bf16[2,1,256,2,256]{4,3,2,1,0:T(2,128)(2,1)}) %tuple.63), branch_computations={%region_18.19_spmd, %region_19.24_spmd} | conditional | flops 682392000 | bytes 27407532 | solution.py:72
  315.8 1.3 copy.139
  319.8 1.4 copy.138
  326.5 14.4 %conditional.10 = (bf16[64,2048]{1,0:T(8,128)(2,1)S(1)}) conditional(s32[]{:T(128)} %convert_element_type.98, () %tuple.56, (s32[]{:T(128)}, bf16[1024,2,256]{2,1,0:T(2,128)(2,1)S(1)}, bf16[2,1,256,2048]{3,2,1,0:T(8,128)(2,1)}, bf16[2,1,256,2,256]{4,3,2,1,0:T(2,128)(2,1)}) %tuple.63), branch_computations={%region_12.13_spmd, %region_13.18_spmd} | conditional | flops 648239488 | bytes 45528136 | solution.py:72
  329.9 1.5 copy.136
  332.2 2.6 bitcast_reduce_fusion.2
  335.3 3.3 fusion.67
  341.7 9.6 %conditional.9 = (bf16[64,2048]{1,0:T(8,128)(2,1)S(1)}) conditional(s32[]{:T(128)} %convert_element_type.97, () %tuple.55, (s32[]{:T(128)}, bf16[1024,2,256]{2,1,0:T(2,128)(2,1)S(1)}, bf16[2,1,256,2048]{3,2,1,0:T(8,128)(2,1)}, bf16[2,1,256,2,256]{4,3,2,1,0:T(2,128)(2,1)}) %tuple.63), branch_computations={%region_6.7_spmd, %region_7.12_spmd} | conditional | flops 614086976 | bytes 25129872 | solution.py:72
  341.8 1.3 copy.135
  345.3 1.5 copy.134
  351.9 13.3 %conditional.8 = (bf16[64,2048]{1,0:T(8,128)(2,1)S(1)}) conditional(s32[]{:T(128)} %convert_element_type.96, () %tuple.53, (s32[]{:T(128)}, bf16[1024,2,256]{2,1,0:T(2,128)(2,1)S(1)}, bf16[2,1,256,2048]{3,2,1,0:T(8,128)(2,1)}, bf16[2,1,256,2,256]{4,3,2,1,0:T(2,128)(2,1)}) %tuple.63), branch_computations={%region_0.0_spmd, %region_1.6_spmd} | conditional | flops 579934272 | bytes 43004164 | solution.py:72
  353.0 1.1 copy.133
  355.2 1.5 copy.132
  357.6 2.6 bitcast_reduce_fusion
  360.5 3.2 fusion.1
  366.9 14.6 %conditional.14 = (bf16[64,2048]{1,0:T(8,128)(2,1)S(1)}) conditional(s32[]{:T(128)} %convert_element_type.102, () %tuple.61, (s32[]{:T(128)}, bf16[1024,2,256]{2,1,0:T(2,128)(2,1)S(1)}, bf16[2,1,256,2048]{3,2,1,0:T(8,128)(2,1)}, bf16[2,1,256,2,256]{4,3,2,1,0:T(2,128)(2,1)}) %tuple.67), branch_computations={%region_36.37_spmd, %region_37.42_spmd} | conditional | flops 648239488 | bytes 45528136 | solution.py:72
  370.3 1.5 copy.144
  372.7 2.6 bitcast_reduce_fusion.6
  375.7 3.3 fusion.199
  382.2 9.8 %conditional.13 = (bf16[64,2048]{1,0:T(8,128)(2,1)S(1)}) conditional(s32[]{:T(128)} %convert_element_type.101, () %tuple.60, (s32[]{:T(128)}, bf16[1024,2,256]{2,1,0:T(2,128)(2,1)S(1)}, bf16[2,1,256,2048]{3,2,1,0:T(8,128)(2,1)}, bf16[2,1,256,2,256]{4,3,2,1,0:T(2,128)(2,1)}) %tuple.67), branch_computations={%region_30.31_spmd, %region_31.36_spmd} | conditional | flops 614086976 | bytes 25129872 | solution.py:72
  382.4 1.3 copy.143
  385.9 1.5 copy.142
  392.7 12.6 %conditional.12 = (bf16[64,2048]{1,0:T(8,128)(2,1)S(1)}) conditional(s32[]{:T(128)} %convert_element_type.100, () %tuple.58, (s32[]{:T(128)}, bf16[1024,2,256]{2,1,0:T(2,128)(2,1)S(1)}, bf16[2,1,256,2048]{3,2,1,0:T(8,128)(2,1)}, bf16[2,1,256,2,256]{4,3,2,1,0:T(2,128)(2,1)}) %tuple.67), branch_computations={%region_24.25_spmd, %region_25.30_spmd} | conditional | flops 579934272 | bytes 40906984 | solution.py:72
  393.8 1.1 copy.141
  396.1 1.5 copy.140
  397.7 2.6 bitcast_reduce_fusion.4
  400.6 3.2 fusion.133
  406.0 1.5 maximum_bitcast_fusion.1
  407.5 1.5 maximum_bitcast_fusion
  (171 shorter events, 49.8 us)
Async XLA Ops:
  6.5 307.3 %all-gather.2.cloned.1.call-start = ((), (), s32[]{:S(2)}) async-start(), calls=%async_computation | async-start | bytes 2113536 | tf_op jit(solution)/shard_map/all_gather | solution.py:82
  321.3 0.9 copy-start.17
  325.8 0.7 copy-start.4
  334.8 4.1 copy-start.14
  334.9 4.1 copy-start
  341.0 0.7 copy-start.6
  351.2 0.7 copy-start.8
  360.2 3.7 copy-start.15
  360.2 3.7 copy-start.1
  365.2 0.7 copy-start.9
  366.2 0.7 copy-start.10
  375.3 4.1 copy-start.16
  375.3 4.1 copy-start.2
  381.5 0.7 copy-start.11
  392.0 0.7 copy-start.12
  392.7 13.3 %copy-start.5 = (bf16[64,2048]{1,0:T(8,128)(2,1)S(1)}, bf16[64,2048]{1,0:T(8,128)(2,1)}, u32[]{:S(2)}) copy-start(bf16[64,2048]{1,0:T(8,128)(2,1)} %copy-done.4) | copy-start | bytes 786436
  392.7 13.3 %copy-start.7 = (bf16[64,2048]{1,0:T(8,128)(2,1)S(1)}, bf16[64,2048]{1,0:T(8,128)(2,1)}, u32[]{:S(2)}) copy-start(bf16[64,2048]{1,0:T(8,128)(2,1)} %copy-done.6) | copy-start | bytes 786436
  400.3 3.7 copy-start.3
  405.3 0.7 copy-start.13
Sparse Core Ops, SparseCore 0:
  9.0 304.6 all-gather.1
where the time goes:
time: 425 us; the launch traced here: 416 us
  waiting for transfers between devices  301 us (71%)
  local copies, waits for them, and re-layouts  39.1 us (9%)
  other arithmetic  30.3 us (7%)
  matrix products  25.6 us (6%)
  between operations  19.2 us (5%)
    all_gather x1, waiting for transfers between devices, per_device(): lax.all_gather(prompt_kv, ('dp', 'tensor'), axis=0, tiled=True)  300 us
    another operation x15, local copies, waits for them, and re-layouts  18.6 us
    reduce_sum x14, other arithmetic, attend_block(): totals = jnp.sum(prompt_weights, axis=-1) + jnp.sum(own_weights, axis=-1)  18 us
    dot_general x7, matrix products, attend_block(): jnp.einsum('tgqd,sgd->gqts', query_heads, prompt_keys, preferred_element_...  12.8 us
  transfers between devices with their start and end apart: 1, of which 1 were waited for; matrix products, arithmetic and copies ran while one was open for 0% of the time, Pallas kernels for 0%

commit v1 on v0

v1 whole, which is shorter than its diff:
```python
import functools
import math

import jax
import jax.numpy as jnp
from jax import lax
from jax.experimental import pallas as pl
from jax.experimental.pallas import tpu as pltpu
from jax.sharding import PartitionSpec as P

MESH = pl.DeviceIdType.MESH
BF16 = jnp.bfloat16
F32 = jnp.float32
HEAD = 128
HEADS = 8
GROUPS = 2
SLOT = 256
PROMPT = 1024
TILE = 256
TOKENS = 64
ROWS = TOKENS * HEADS
SCALE = math.log2(math.e) / math.sqrt(HEAD)
NEG = -1e30


def turn(index, step):
    return lax.rem(index + step, 4)


def coordinates():
    dp, tensor = lax.axis_index("dp"), lax.axis_index("tensor")
    core = lax.rem(dp, 2)
    z = lax.rem(lax.div(dp, 2), 4)
    x = lax.rem(lax.div(dp, 8), 4)
    y = lax.div(dp, 32) * 2 + tensor
    return x, y, z, core


def device(x, y, z, core):
    return (((lax.div(y, 2) * 4 + x) * 4 + z) * 2 + core, lax.rem(y, 2))


def ring_hops(step):
    return min(step, 4 - step)


def remote(src, dst, send, recv, target):
    return pltpu.make_async_remote_copy(
        src_ref=src, dst_ref=dst, send_sem=send, recv_sem=recv, device_id=target, device_id_type=MESH
    )


def landed(ref, sem):
    pltpu.make_async_copy(ref, ref, sem).wait()


def gather_kernel(shard, out, kv, other, stage, s0, r0, s1, r1, s2, r2, s3, r3):
    x, y, z, core = coordinates()
    tensor = lax.rem(y, 2)
    outer = jnp.where(core == 0, z, x)
    inner = jnp.where(core == 0, x, z)

    def place(outer_, y_, inner_):
        return device(
            jnp.where(core == 0, inner_, outer_), y_, jnp.where(core == 0, outer_, inner_), core
        )

    partner = device(x, y, z, 1 - core)
    plane = [(dy, d) for dy in range(4) for d in range(4) if dy or d]
    plane.sort(key=lambda step: -ring_hops(step[0]) - ring_hops(step[1]))
    plane_devices = [place(outer, turn(y, dy), turn(inner, d)) for dy, d in plane]
    line_devices = {d: place(turn(outer, d), y, inner) for d in (1, 2, 3)}
    peers = plane_devices + list(line_devices.values()) + [partner]
    barrier = pltpu.get_barrier_semaphore()
    for peer in peers:
        pl.semaphore_signal(barrier, inc=1, device_id=peer, device_id_type=MESH)
    pl.semaphore_wait(barrier, len(peers))

    remote(shard.at[1 - core], other, s0.at[0], r0.at[0], partner).start()
    landed(other, r0.at[0])
    mine, theirs = shard[core], other[...]
    stage[:, 0] = jnp.concatenate([mine[:, 0:8], theirs[:, 0:8]], 1)
    stage[:, 1] = jnp.concatenate([mine[:, 8:16], theirs[:, 8:16]], 1)
    slot = inner * 4 + y
    kv[core, outer, :, slot] = stage[tensor]
    for (dy, _), target in zip(plane, plane_devices):
        to = lax.rem(turn(y, dy), 2)
        remote(stage.at[to], kv.at[core, outer, :, slot], s1.at[0], r1.at[0], target).start()
    landed(kv.at[core, outer, :, 0:15], r1.at[0])
    block = kv.at[core, outer]
    for d in (1, 3, 2):
        remote(block, block, s2.at[d], r2.at[d], line_devices[d]).start()
    remote(block, block, s3.at[0], r3.at[0], partner).start()
    for d in (1, 3, 2):
        block = kv.at[core, turn(outer, 4 - d)]
        landed(block, r2.at[d])
        remote(block, block, s3.at[d], r3.at[d], partner).start()
    for d in range(4):
        landed(kv.at[1 - core, 0], r3.at[d])
    landed(other, s0.at[0])
    landed(kv.at[core, outer, :, 0:15], s1.at[0])
    for d in range(4):
        if d:
            landed(block, s2.at[d])
        landed(block, s3.at[d])
    out[...] = kv[...]


def gather(prompt):
    shard = prompt.reshape(8, 2, 2, 2, HEAD).transpose(3, 2, 1, 0, 4).reshape(2, 2, 16, HEAD)
    vmem, dma = pltpu.VMEM, pltpu.SemaphoreType.DMA
    shape = (GROUPS, 4, 2, 16, 16, HEAD)
    return pl.pallas_call(
        gather_kernel,
        in_specs=[pl.BlockSpec(memory_space=vmem)],
        out_specs=pl.BlockSpec(memory_space=vmem),
        out_shape=jax.ShapeDtypeStruct(shape, BF16),
        scratch_shapes=[
            vmem(shape, BF16),
            vmem((2, 16, HEAD), BF16),
            vmem((2, 2, 16, HEAD), BF16),
            dma((1,)), dma((1,)), dma((1,)), dma((1,)),
            dma((4,)), dma((4,)), dma((4,)), dma((4,)),
        ],
        compiler_params=pltpu.CompilerParams(
            collective_id=0, has_side_effects=True, vmem_limit_bytes=40 << 20
        ),
    )(shard)


def attend_kernel(lengths, q, own, prompt, out, scores_a, scores_b, tops):
    length0, length1 = lengths[0], lengths[1]
    count0 = lax.div(length0 + TOKENS - 1, TOKENS)
    count1 = lax.div(length1 + TOKENS - 1, TOKENS)
    units = 2 * (count0 + count1)
    ones = jnp.ones((TILE, HEAD), BF16)

    def locate(unit):
        s = (unit >= 2 * count0).astype(jnp.int32)
        rest = unit - s * 2 * count0
        count = jnp.where(s == 0, count0, count1)
        g = (rest >= count).astype(jnp.int32)
        token = pl.multiple_of((rest - g * count) * TOKENS, TOKENS)
        return s, g, token, jnp.where(s == 0, length0, length1)

    def head_columns(g, head):
        return pl.ds(pl.multiple_of(g * HEADS * HEAD + head * HEAD, HEAD), HEAD)

    def step(current, scores_now, following, scores_next):
        if following is not None:
            s, g, token, length = locate(following)
            rows = pl.ds(token, TOKENS)
            queries = jnp.concatenate([q[s, rows, head_columns(g, h)] for h in range(HEADS)], 0)
            part_top = None
        if current is not None:
            s_now, g_now, token_now, length_now = locate(current)
            top = tops[...]
            top = jnp.concatenate([top, top], 1)
            total = jnp.zeros((ROWS, 2 * HEAD), F32)
        for k in range(5):
            keys = slice(k * TILE, (k + 1) * TILE)
            if following is not None:
                source = prompt[g, k, 0].reshape(TILE, HEAD) if k < 4 else own[s, g, 0]
                part = lax.dot_general(
                    queries, source, (((1,), (1,)), ((), ())), preferred_element_type=F32
                )
                if k == 4:
                    position = token + lax.rem(lax.broadcasted_iota(jnp.int32, (ROWS, TILE), 0), TOKENS)
                    key = lax.broadcasted_iota(jnp.int32, (ROWS, TILE), 1)
                    part = jnp.where((key <= position) & (key < length), part, NEG)
                scores_next[:, keys] = part
                part = jnp.maximum(part[:, :HEAD], part[:, HEAD:])
                part_top = part if part_top is None else jnp.maximum(part_top, part)
            if current is not None:
                weights = jnp.exp2((scores_now[:, keys] - top) * SCALE).astype(BF16)
                source = prompt[g_now, k, 1].reshape(TILE, HEAD) if k < 4 else own[s_now, g_now, 1]
                total += jnp.dot(
                    weights, jnp.concatenate([source, ones], 1), preferred_element_type=F32
                )
        if following is not None:
            tops[...] = jnp.broadcast_to(jnp.max(part_top, -1, keepdims=True), (ROWS, HEAD))
        if current is not None:
            result = total[:, :HEAD] / total[:, HEAD:]
            position = token_now + lax.rem(lax.broadcasted_iota(jnp.int32, (ROWS, HEAD), 0), TOKENS)
            result = jnp.where(position < length_now, result, 0.0).astype(BF16)
            for h in range(HEADS):
                out[s_now, pl.ds(token_now, TOKENS), head_columns(g_now, h)] = result[
                    h * TOKENS : (h + 1) * TOKENS
                ]

    step(None, None, 0, scores_a)

    @pl.loop(0, lax.div(units, 2))
    def _(pair):
        unit = 2 * pair
        step(unit, scores_a, unit + 1, scores_b)
        step(unit + 1, scores_b, jnp.minimum(unit + 2, units - 1), scores_a)

    for s, count in ((0, count0), (1, count1)):

        @pl.loop(count, SLOT // TOKENS)
        def _(i):
            out[s, pl.ds(pl.multiple_of(i * TOKENS, TOKENS), TOKENS), :] = jnp.zeros(
                (TOKENS, GROUPS * HEADS * HEAD), BF16
            )


def attend(lengths, queries, own, prompt):
    vmem = pltpu.VMEM
    return pl.pallas_call(
        attend_kernel,
        in_specs=[pl.BlockSpec(memory_space=pltpu.SMEM)] + [pl.BlockSpec(memory_space=vmem)] * 3,
        out_specs=pl.BlockSpec(memory_space=vmem),
        out_shape=jax.ShapeDtypeStruct(queries.shape, BF16),
        scratch_shapes=[
            vmem((ROWS, PROMPT + SLOT), F32),
            vmem((ROWS, PROMPT + SLOT), F32),
            vmem((ROWS, HEAD), F32),
        ],
        compiler_params=pltpu.CompilerParams(vmem_limit_bytes=50 << 20),
    )(lengths, queries, own, prompt)


def per_device(queries, trace_kv, lengths, prompt_kv):
    prompt = gather(prompt_kv)
    own = trace_kv[:, 0].reshape(2, SLOT, 2, GROUPS, HEAD).transpose(0, 3, 2, 1, 4)
    out = attend(lengths[:, 0], queries[:, 0], own, prompt)
    return out[:, None]


def solution(mesh):
    placed = (
        P(None, "dp", None, "tensor"),
        P(None, "dp", None, None, "tensor"),
        P(None, "dp"),
        P(("dp", "tensor"), None, None),
    )
    return jax.shard_map(
        per_device,
        mesh=mesh,
        in_specs=placed,
        out_specs=P(None, "dp", None, "tensor"),
        check_vma=False,
    )
```

time: 425 us -> 38.1 us (0.09); the launches traced: 416 us -> 37.9 us
  waiting for transfers between devices: 301 us -> 0 us
  local copies, waits for them, and re-layouts: 39.1 us -> 2.46 us
  Pallas kernels: 0 us -> 35.4 us
  other arithmetic: 30.3 us -> 0 us
  matrix products: 25.6 us -> 0 us
  between operations: 19.2 us -> 0.05 us
    all_gather x1 -> x0, waiting for transfers between devices: 300 us -> none  [per_device(): lax.all_gather(prompt_kv, ('dp', 'tensor'), axis=0, tiled=True)]
    pallas_call x0 -> x2, Pallas kernels: none -> 35.4 us  [the longest x1 21 us: gather(): pl.pallas_call(gather_kernel, in_specs=[pl.BlockSpec(memory_space=vmem)],...]
    dot_general x28 -> x0, matrix products: 25.6 us -> none  [the longest x7 12.8 us: attend_block(): jnp.einsum('tgqd,sgd->gqts', query_heads, prompt_keys, preferred_element_...]
    another operation x15 -> x1, local copies, waits for them, and re-layouts: 18.6 us -> 0.27 us  [per_device(): trace_kv[:, 0].reshape(2, SLOT, 2, GROUPS, HEAD).transpose(0, 3, 2, 1, 4)]
    reduce_sum x14 -> x0, other arithmetic: 18 us -> none  [attend_block(): totals = jnp.sum(prompt_weights, axis=-1) + jnp.sum(own_weights, axis=-1)]
    lt x12 -> x0, other arithmetic: 7.79 us -> none  [the longest x7 4.55 us: attend_block(): result = jnp.where(token_pos[:, None] < length, result, 0.0)]
    cond x30 -> x0, local copies, waits for them, and re-layouts: 7.14 us -> none
    slice x21 -> x0, local copies, waits for them, and re-layouts: 4.41 us -> none  [the longest x7 2.87 us: attend_block(): prompt_cols[:, 1].reshape(prompt_cols.shape[0], groups, HEAD)]
  transfers between devices with their start and end apart: 1 -> 0, of which waited for: 1 -> 0; matrix products, arithmetic and copies ran while one was open for 0% -> 0% of each run, Pallas kernels for 0% -> 0%
where the time goes in v1:
time: 38.1 us; the launch traced here: 37.9 us
  Pallas kernels  35.4 us (93%)
  local copies, waits for them, and re-layouts  2.46 us (6%)
    pallas_call x1, Pallas kernels, gather(): pl.pallas_call(gather_kernel, in_specs=[pl.BlockSpec(memory_space=vmem)],...  21 us
    pallas_call x1, Pallas kernels, attend(): pl.pallas_call(attend_kernel, in_specs=[pl.BlockSpec(memory_space=pltpu.S...  14.4 us
    unnamed x5, local copies, waits for them, and re-layouts  1.3 us
    reshape x2, local copies, waits for them, and re-layouts, gather(): prompt.reshape(8, 2, 2, 2, HEAD).transpose(3, 2, 1, 0, 4)  0.89 us

profile of v1, /device:TPU:1, one launch (start us, length us, event | category | flops | bytes accessed | tf_op | source)
XLA Modules:
  0.0 37.9 jit_solution(16502816418888439914)
XLA Ops:
  0.0 0.0 copy-start.1
  0.0 0.0 copy-start
  0.0 0.9 %reshape.6 = bf16[8,2,2,2,128]{4,3,2,1,0:T(2,128)(2,1)S(1)} reshape(bf16[8,2,512]{2,1,0:T(2,128)(2,1)} %param.7) | data formatting | bytes 32768 | tf_op jit(solution)/shard_map/reshape | solution.py:110
  0.9 1.3 %copy.7 = bf16[2,1,256,2,256]{2,4,3,0,1:T(8,128)(2,1)S(1)} copy(bf16[2,1,256,2,256]{4,3,2,1,0:T(2,128)(2,1)} %param.5) | data formatting | bytes 1048576 | tf_op args[1]
  2.2 0.3 copy.8
  2.5 21.0 %shard_map.46.prompt = bf16[2,4,2,16,16,128]{5,4,3,2,1,0:T(8,128)(2,1)S(1)} custom-call(bf16[2,2,16,128]{3,2,1,0:T(8,128)(2,1)S(1)} %bitcast.14), custom_call_target="tpu_custom_call" | custom-call | tf_op jit(solution)/shard_map/pallas_call | solution.py:113
  23.5 0.0 copy-done.1
  23.5 0.0 copy-done
  23.5 14.4 %shard_map.47 = bf16[2,256,2048]{2,1,0:T(8,128)(2,1)} custom-call(s32[2]{0:T(128)S(1)} %bitcast.15, bf16[2,256,2048]{2,1,0:T(8,128)(2,1)S(1)} %bitcast.12, bf16[2,2,2,256,128]{4,3,2,1,0:T(8,128)(2,1)S(1)} %bitcast.13, bf16[2,4,2,16,16,128]{5,4,3,2,1,0:T(8,128)(2,1)S(1)} %shard_map.46.prompt), custom_call_target="tpu_custom_call" | custom-call | tf_op jit(solution)/shard_map/pallas_call | solution.py:210
  (1 shorter events, 0.0 us)
Async XLA Ops:
  0.0 23.5 %copy-start.1 = (s32[2,1]{0,1:T(1,128)S(1)}, s32[2,1]{0,1:T(1,128)}, u32[]{:S(2)}) copy-start(s32[2,1]{0,1:T(1,128)} %param.6) | copy-start | bytes 28
  0.0 23.5 %copy-start = (bf16[2,1,256,2048]{3,2,1,0:T(8,128)(2,1)S(1)}, bf16[2,1,256,2048]{3,2,1,0:T(8,128)(2,1)}, u32[]{:S(2)}) copy-start(bf16[2,1,256,2048]{3,2,1,0:T(8,128)(2,1)} %param.4) | copy-start | bytes 6291460

commit v2 on v1

v2 whole, which is shorter than its diff:
```python
import math

import jax
import jax.numpy as jnp
from jax import lax
from jax.experimental import pallas as pl
from jax.experimental.pallas import tpu as pltpu
from jax.sharding import PartitionSpec as P

MESH = pl.DeviceIdType.MESH
BF16 = jnp.bfloat16
F32 = jnp.float32
HEAD = 128
HEADS = 8
GROUPS = 2
SLOT = 256
PROMPT = 1024
TILE = 256
TOKENS = 64
ROWS = TOKENS * HEADS
PAIRS = HEADS // 2
SCALE = math.log2(math.e) / math.sqrt(HEAD)
NEG = -1e30
PLANES = ((0, 1), (3, 2))


def turn(index, step):
    return lax.rem(index + step, 4)


def coordinates():
    dp, tensor = lax.axis_index("dp"), lax.axis_index("tensor")
    core = lax.rem(dp, 2)
    z = lax.rem(lax.div(dp, 2), 4)
    x = lax.rem(lax.div(dp, 8), 4)
    y = lax.div(dp, 32) * 2 + tensor
    return x, y, z, core


def device(x, y, z, core):
    return (((lax.div(y, 2) * 4 + x) * 4 + z) * 2 + core, lax.rem(y, 2))


def ring_hops(step):
    return min(step, 4 - step)


def remote(src, dst, send, recv, target):
    return pltpu.make_async_remote_copy(
        src_ref=src, dst_ref=dst, send_sem=send, recv_sem=recv, device_id=target, device_id_type=MESH
    )


def landed(ref, sem):
    pltpu.make_async_copy(ref, ref, sem).wait()


def head_columns(g, head):
    return pl.ds(pl.multiple_of(g * HEADS * HEAD + head * HEAD, HEAD), HEAD)


def first_kernel(
    lengths_hbm, shard_hbm, queries, trace_kv, out_hbm, kv_out, later_out,
    lengths, blocks, kv, shard, stage, q, raw, own, later, out, scores, tops,
    s1, r1, s3, r3, local,
):
    x, y, z, core = coordinates()
    tensor = lax.rem(y, 2)
    partner = device(x, y, z, 1 - core)
    away = [(a, b, c) for a in range(4) for b in range(4) for c in range(4) if a or b or c]
    away.sort(key=lambda step: -sum(map(ring_hops, step)))
    chips = [device(turn(x, a), turn(y, b), turn(z, c), core) for a, b, c in away]
    barrier = pltpu.get_barrier_semaphore()
    for peer in chips + [partner]:
        pl.semaphore_signal(barrier, inc=1, device_id=peer, device_id_type=MESH)
    load_shard = pltpu.make_async_copy(shard_hbm, shard, local.at[3])
    load_shard.start()
    load_lengths = pltpu.make_async_copy(lengths_hbm, lengths, local.at[6])
    load_lengths.start()
    load_q = pltpu.make_async_copy(queries.at[0], q, local.at[0])
    load_own = pltpu.make_async_copy(trace_kv, raw, local.at[1])
    load_q.start()
    load_own.start()
    load_shard.wait()
    for t in range(2):
        for k in range(2):
            columns = t * 2 * HEAD
            stage[t, k] = jnp.concatenate(
                [shard[:, k, columns : columns + HEAD], shard[:, k, columns + HEAD : columns + 2 * HEAD]], 0
            )
    here = x * 16 + y * 4 + z
    pl.semaphore_wait(barrier, len(chips) + 1)
    for k in range(2):
        for (_, b, _), target in zip(away, chips):
            to = lax.rem(turn(y, b), 2)
            remote(stage.at[to, k], blocks.at[core, k, here], s1.at[k], r1.at[k, x], target).start()
    for k in range(2):
        blocks[core, k, here] = stage[tensor, k]

    def scores_of(g, column, keys, mask=None):
        for j in range(PAIRS):
            pair = jnp.concatenate([q[:, head_columns(g, 2 * j)], q[:, head_columns(g, 2 * j + 1)]], 0)
            tile = lax.dot_general(pair, keys, (((1,), (1,)), ((), ())), preferred_element_type=F32)
            if mask is not None:
                tile = jnp.where(mask, tile, NEG)
            scores[g * PAIRS + j, :, column * TILE : (column + 1) * TILE] = tile
            tile = jnp.maximum(tile[:, :HEAD], tile[:, HEAD:])
            if mask is None:
                tile = jnp.maximum(tops[g * PAIRS + j], tile)
            tops[g * PAIRS + j] = tile

    load_own.wait()
    for s, target in ((0, own), (1, later)):
        for g in range(GROUPS):
            for k in range(2):
                target[g, k] = raw[s, :, k, g * HEAD : (g + 1) * HEAD]
    keep_later = pltpu.make_async_copy(later, later_out, local.at[4])
    keep_later.start()
    load_q.wait()
    load_lengths.wait()
    length = lengths[0]
    position = lax.rem(lax.broadcasted_iota(jnp.int32, (2 * SLOT, TILE), 0), SLOT)
    key = lax.broadcasted_iota(jnp.int32, (2 * SLOT, TILE), 1)
    allowed = (key <= position) & (key < length)

    @pl.loop(0, GROUPS)
    def _(g):
        scores_of(g, 4, own[g, 0], allowed)

    def group(side, k, d):
        return blocks.at[side, k, pl.ds(pl.multiple_of(turn(x, d) * 16, 16), 16)]

    def arrange(side, column, k):
        for g in range(GROUPS):
            rows = [group(side, k, d)[:, g * 8 : (g + 1) * 8].reshape(TILE // 2, HEAD) for d in PLANES[column % 2]]
            kv[g, column, k] = jnp.concatenate(rows, 0)

    def collect(k, column):
        for d in PLANES[column]:
            if d:
                landed(group(core, k, d), r1.at[k, turn(x, d)])
            else:
                landed(blocks.at[core, k, 0:15], r1.at[k, x])
            remote(group(core, k, d), group(core, k, d), s3.at[k, d], r3.at[k, d], partner).start()
        arrange(core, column, k)

    def collect_partner(k, column):
        for d in PLANES[column - 2]:
            landed(group(1 - core, k, d), r3.at[k, d])
        arrange(1 - core, column, k)

    def prompt_scores(column):
        @pl.loop(0, GROUPS)
        def _(g):
            scores_of(g, column, kv[g, column, 0])

    for column in (0, 1):
        collect(0, column)
    for column in (0, 1):
        prompt_scores(column)
    collect_partner(0, 2)
    prompt_scores(2)
    for column in (0, 1):
        collect(1, column)
    collect_partner(0, 3)
    prompt_scores(3)
    for pair in range(GROUPS * PAIRS):
        tops[pair] = jnp.broadcast_to(jnp.max(tops[pair], -1, keepdims=True), (2 * SLOT, HEAD))
    for column in (2, 3):
        collect_partner(1, column)
    keep = pltpu.make_async_copy(kv, kv_out, local.at[2])
    keep.start()

    ones = jnp.ones((TILE, HEAD), BF16)

    @pl.loop(0, GROUPS * PAIRS)
    def _(pair):
        g = lax.div(pair, PAIRS)
        top = jnp.concatenate([tops[pair], tops[pair]], 1)
        total = jnp.zeros((2 * SLOT, 2 * HEAD), F32)
        for column in range(5):
            tile = scores[pair, :, column * TILE : (column + 1) * TILE]
            weights = jnp.exp2((tile - top) * SCALE).astype(BF16)
            values = kv[g, column, 1] if column < 4 else own[g, 1]
            total += jnp.dot(weights, jnp.concatenate([values, ones], 1), preferred_element_type=F32)
        result = total[:, :HEAD] / total[:, HEAD:]
        result = jnp.where(position[:, :HEAD] < length, result, 0.0).astype(BF16)
        columns = pl.ds(pl.multiple_of(pair * 2 * HEAD, 2 * HEAD), 2 * HEAD)
        out[:, columns] = jnp.concatenate([result[:SLOT], result[SLOT:]], 1)
        pltpu.make_async_copy(out.at[:, columns], out_hbm.at[:, columns], local.at[5]).start()

    keep.wait()
    keep_later.wait()
    landed(out, local.at[5])
    for k in range(2):
        landed(blocks.at[core, k, 0:63], s1.at[k])
        for d in range(4):
            landed(group(core, k, d), s3.at[k, d])


def first(lengths, shard, queries, trace_kv):
    vmem, dma = pltpu.VMEM, pltpu.SemaphoreType.DMA
    gathered = (GROUPS, 4, 2, TILE, HEAD)
    columns = GROUPS * HEADS * HEAD
    own = (GROUPS, 2, SLOT, HEAD)
    return pl.pallas_call(
        first_kernel,
        in_specs=[pl.BlockSpec(memory_space=pltpu.HBM)] * 4,
        out_specs=[pl.BlockSpec(memory_space=pltpu.HBM)] * 3,
        out_shape=[
            jax.ShapeDtypeStruct((SLOT, columns), BF16),
            jax.ShapeDtypeStruct(gathered, BF16),
            jax.ShapeDtypeStruct(own, BF16),
        ],
        scratch_shapes=[
            pltpu.SMEM((2,), jnp.int32),
            vmem((2, 2, 64, 16, HEAD), BF16),
            vmem(gathered, BF16),
            vmem((8, 2, 2 * GROUPS * HEAD), BF16),
            vmem((2, 2, 16, HEAD), BF16),
            vmem((SLOT, columns), BF16),
            vmem((2, SLOT, 2, GROUPS * HEAD), BF16),
            vmem(own, BF16),
            vmem(own, BF16),
            vmem((SLOT, columns), BF16),
            vmem((2 * PAIRS, 2 * SLOT, PROMPT + SLOT), F32),
            vmem((2 * PAIRS, 2 * SLOT, HEAD), F32),
            dma((2,)), dma((2, 4)), dma((2, 4)), dma((2, 4)), dma((7,)),
        ],
        compiler_params=pltpu.CompilerParams(
            collective_id=0, has_side_effects=True, vmem_limit_bytes=44 << 20
        ),
    )(lengths, shard, queries, trace_kv)


def second_kernel(lengths, q, own, prompt, done, out, scores_a, scores_b, tops, result_ref, local):
    carry_over = pltpu.make_async_copy(done, out.at[0], local.at[0])
    carry_over.start()
    length = lengths[1]
    count = lax.div(length + TOKENS - 1, TOKENS)
    units = 2 * count
    ones = jnp.ones((TILE, HEAD), BF16)

    def locate(unit):
        g = (unit >= count).astype(jnp.int32)
        return g, pl.multiple_of((unit - g * count) * TOKENS, TOKENS)

    def step(current, scores_now, following, scores_next):
        if following is not None:
            g, token = locate(following)
            rows = pl.ds(token, TOKENS)
            queries = jnp.concatenate([q[1, rows, head_columns(g, h)] for h in range(HEADS)], 0)
            part_top = None
        if current is not None:
            g_now, token_now = locate(current)
            top = tops[...]
            top = jnp.concatenate([top, top], 1)
            total = jnp.zeros((ROWS, 2 * HEAD), F32)
        for k in range(5):
            keys = slice(k * TILE, (k + 1) * TILE)
            if following is not None:
                source = prompt[g, k, 0] if k < 4 else own[g, 0]
                part = lax.dot_general(
                    queries, source, (((1,), (1,)), ((), ())), preferred_element_type=F32
                )
                if k == 4:
                    position = token + lax.rem(lax.broadcasted_iota(jnp.int32, (ROWS, TILE), 0), TOKENS)
                    key = lax.broadcasted_iota(jnp.int32, (ROWS, TILE), 1)
                    part = jnp.where((key <= position) & (key < length), part, NEG)
                scores_next[:, keys] = part
                part = jnp.maximum(part[:, :HEAD], part[:, HEAD:])
                part_top = part if part_top is None else jnp.maximum(part_top, part)
            if current is not None:
                weights = jnp.exp2((scores_now[:, keys] - top) * SCALE).astype(BF16)
                source = prompt[g_now, k, 1] if k < 4 else own[g_now, 1]
                total += jnp.dot(
                    weights, jnp.concatenate([source, ones], 1), preferred_element_type=F32
                )
        if following is not None:
            tops[...] = jnp.broadcast_to(jnp.max(part_top, -1, keepdims=True), (ROWS, HEAD))
        if current is not None:
            result = total[:, :HEAD] / total[:, HEAD:]
            position = token_now + lax.rem(lax.broadcasted_iota(jnp.int32, (ROWS, HEAD), 0), TOKENS)
            result = jnp.where(position < length, result, 0.0).astype(BF16)
            for h in range(HEADS):
                result_ref[pl.ds(token_now, TOKENS), head_columns(g_now, h)] = result[
                    h * TOKENS : (h + 1) * TOKENS
                ]

    @pl.loop(count, SLOT // TOKENS)
    def _(i):
        result_ref[pl.ds(pl.multiple_of(i * TOKENS, TOKENS), TOKENS), :] = jnp.zeros(
            (TOKENS, GROUPS * HEADS * HEAD), BF16
        )

    step(None, None, 0, scores_a)

    @pl.loop(0, count)
    def _(pair):
        unit = 2 * pair
        step(unit, scores_a, unit + 1, scores_b)
        step(unit + 1, scores_b, jnp.minimum(unit + 2, units - 1), scores_a)

    store = pltpu.make_async_copy(result_ref, out.at[1], local.at[1])
    store.start()
    carry_over.wait()
    store.wait()


def second(lengths, queries, own, prompt, done):
    vmem = pltpu.VMEM
    return pl.pallas_call(
        second_kernel,
        in_specs=[pl.BlockSpec(memory_space=pltpu.SMEM)] + [pl.BlockSpec(memory_space=vmem)] * 4,
        out_specs=pl.BlockSpec(memory_space=pltpu.HBM),
        out_shape=jax.ShapeDtypeStruct(queries.shape, BF16),
        scratch_shapes=[
            vmem((ROWS, PROMPT + SLOT), F32),
            vmem((ROWS, PROMPT + SLOT), F32),
            vmem((ROWS, HEAD), F32),
            vmem((SLOT, GROUPS * HEADS * HEAD), BF16),
            pltpu.SemaphoreType.DMA((2,)),
        ],
        compiler_params=pltpu.CompilerParams(vmem_limit_bytes=40 << 20),
    )(lengths, queries, own, prompt, done)


def per_device(queries, trace_kv, lengths, prompt_kv):
    lengths, queries = lengths[:, 0], queries[:, 0]
    arguments = (lengths, prompt_kv, queries, trace_kv[:, 0])
    done, prompt, own = first(*(pltpu.with_memory_space_constraint(a, pltpu.HBM) for a in arguments))
    return second(lengths, queries, own, prompt, done)[:, None]


def solution(mesh):
    placed = (
        P(None, "dp", None, "tensor"),
        P(None, "dp", None, None, "tensor"),
        P(None, "dp"),
        P(("dp", "tensor"), None, None),
    )
    return jax.shard_map(
        per_device,
        mesh=mesh,
        in_specs=placed,
        out_specs=P(None, "dp", None, "tensor"),
        check_vma=False,
    )
```

time: 38.1 us -> 32.8 us (0.86)
  Pallas kernels: 35.4 us -> 32.7 us
  local copies, waits for them, and re-layouts: 2.46 us -> 0.01 us
    pallas_call x2, Pallas kernels: 35.4 us -> 32.7 us  [the longest x1 25.4 us: first(): pl.pallas_call(first_kernel, in_specs=[pl.BlockSpec(memory_space=pltpu.HB...]
    unnamed x5 -> x4, local copies, waits for them, and re-layouts: 1.3 us -> 0.01 us
    reshape x2 -> x0, local copies, waits for them, and re-layouts: 0.89 us -> none  [gather(): prompt.reshape(8, 2, 2, 2, HEAD).transpose(3, 2, 1, 0, 4)]
where the time goes in v2:
time: 32.8 us; the launch traced here: 32.7 us
  Pallas kernels  32.7 us (100%)
    pallas_call x1, Pallas kernels, first(): pl.pallas_call(first_kernel, in_specs=[pl.BlockSpec(memory_space=pltpu.HB...  25.4 us
    pallas_call x1, Pallas kernels, second(): pl.pallas_call(second_kernel, in_specs=[pl.BlockSpec(memory_space=pltpu.S...  7.26 us

profile of v2, /device:TPU:1, one launch (start us, length us, event | category | flops | bytes accessed | tf_op | source)
XLA Modules:
  0.0 32.7 jit_solution(8437922882629767789)
XLA Ops:
  0.0 0.0 copy-start.1
  0.0 0.0 copy-start
  0.0 25.4 %shard_map.46 = (bf16[256,2048]{1,0:T(8,128)(2,1)S(1)}, bf16[2,4,2,256,128]{4,3,2,1,0:T(8,128)(2,1)S(1)}, bf16[2,2,256,128]{3,2,1,0:T(8,128)(2,1)S(1)}) custom-call(s32[2]{0:T(128)} %bitcast.8, bf16[8,2,512]{2,1,0:T(2,128)(2,1)} %shard_hbm.1, bf16[2,256,2048]{2,1,0:T(8,128)(2,1)} %bitcast.6, bf16[2,256,2,256]{3,2,1,0:T(2,128)(2,1)} %bitcast.10), custom_call_target="tpu_custom_call" | custom-call | tf_op jit(solution)/shard_map/pallas_call | solution.py:206
  25.4 0.0 copy-done.1
  25.4 0.0 copy-done
  25.4 7.3 %shard_map.47 = bf16[2,256,2048]{2,1,0:T(8,128)(2,1)} custom-call(s32[2]{0:T(128)S(1)} %bitcast.9, bf16[2,256,2048]{2,1,0:T(8,128)(2,1)S(1)} %bitcast.7, bf16[2,2,256,128]{3,2,1,0:T(8,128)(2,1)S(1)} %get-tuple-element.8.own, bf16[2,4,2,256,128]{4,3,2,1,0:T(8,128)(2,1)S(1)} %get-tuple-element.9.prompt, bf16[256,2048]{1,0:T(8,128)(2,1)S(1)} %get-tuple-element.10.done), custom_call_target="tpu_custom_call" | custom-call | tf_op jit(solution)/shard_map/pallas_call | solution.py:312
Async XLA Ops:
  0.0 25.4 %copy-start.1 = (s32[2,1]{0,1:T(1,128)S(1)}, s32[2,1]{0,1:T(1,128)}, u32[]{:S(2)}) copy-start(s32[2,1]{0,1:T(1,128)} %param.6) | copy-start | bytes 28
  0.0 25.4 %copy-start = (bf16[2,1,256,2048]{3,2,1,0:T(8,128)(2,1)S(1)}, bf16[2,1,256,2048]{3,2,1,0:T(8,128)(2,1)}, u32[]{:S(2)}) copy-start(bf16[2,1,256,2048]{3,2,1,0:T(8,128)(2,1)} %param.4) | copy-start | bytes 6291460

commit v3 on v2

--- a/solution.py
+++ b/solution.py
@@ -67,14 +67,23 @@
     x, y, z, core = coordinates()
     tensor = lax.rem(y, 2)
     partner = device(x, y, z, 1 - core)
+    load_shard = pltpu.make_async_copy(shard_hbm, shard, local.at[3])
+    load_shard.start()
     away = [(a, b, c) for a in range(4) for b in range(4) for c in range(4) if a or b or c]
     away.sort(key=lambda step: -sum(map(ring_hops, step)))
-    chips = [device(turn(x, a), turn(y, b), turn(z, c), core) for a, b, c in away]
+    rows = [turn(y, b) for b in range(4)]
+    row_tensor = [lax.rem(row, 2) for row in rows]
+    row_base = [lax.div(row, 2) * 32 for row in rows]
+    column_base = [[turn(x, a) * 8 + turn(z, c) * 2 + core for c in range(4)] for a in range(4)]
+
+    def chip(step):
+        a, b, c = step
+        return row_base[b] + column_base[a][c], row_tensor[b]
+
     barrier = pltpu.get_barrier_semaphore()
-    for peer in chips + [partner]:
-        pl.semaphore_signal(barrier, inc=1, device_id=peer, device_id_type=MESH)
-    load_shard = pltpu.make_async_copy(shard_hbm, shard, local.at[3])
-    load_shard.start()
+    for step in away:
+        pl.semaphore_signal(barrier, inc=1, device_id=chip(step), device_id_type=MESH)
+    pl.semaphore_signal(barrier, inc=1, device_id=partner, device_id_type=MESH)
     load_lengths = pltpu.make_async_copy(lengths_hbm, lengths, local.at[6])
     load_lengths.start()
     load_q = pltpu.make_async_copy(queries.at[0], q, local.at[0])
@@ -89,11 +98,11 @@
                 [shard[:, k, columns : columns + HEAD], shard[:, k, columns + HEAD : columns + 2 * HEAD]], 0
             )
     here = x * 16 + y * 4 + z
-    pl.semaphore_wait(barrier, len(chips) + 1)
+    pl.semaphore_wait(barrier, len(away) + 1)
     for k in range(2):
-        for (_, b, _), target in zip(away, chips):
-            to = lax.rem(turn(y, b), 2)
-            remote(stage.at[to, k], blocks.at[core, k, here], s1.at[k], r1.at[k, x], target).start()
+        for step in away:
+            block = stage.at[row_tensor[step[1]], k]
+            remote(block, blocks.at[core, k, here], s1.at[k], r1.at[k, x], chip(step)).start()
     for k in range(2):
         blocks[core, k, here] = stage[tensor, k]
 
@@ -163,9 +172,10 @@
     for column in (0, 1):
         collect(1, column)
     collect_partner(0, 3)
-    prompt_scores(3)
-    for pair in range(GROUPS * PAIRS):
-        tops[pair] = jnp.broadcast_to(jnp.max(tops[pair], -1, keepdims=True), (2 * SLOT, HEAD))
+    for g in range(GROUPS):
+        scores_of(g, 3, kv[g, 3, 0])
+        for pair in range(g * PAIRS, (g + 1) * PAIRS):
+            tops[pair] = jnp.broadcast_to(jnp.max(tops[pair], -1, keepdims=True), (2 * SLOT, HEAD))
     for column in (2, 3):
         collect_partner(1, column)
     keep = pltpu.make_async_copy(kv, kv_out, local.at[2])
@@ -173,21 +183,25 @@
 
     ones = jnp.ones((TILE, HEAD), BF16)
 
-    @pl.loop(0, GROUPS * PAIRS)
-    def _(pair):
-        g = lax.div(pair, PAIRS)
-        top = jnp.concatenate([tops[pair], tops[pair]], 1)
-        total = jnp.zeros((2 * SLOT, 2 * HEAD), F32)
+    @pl.loop(0, GROUPS * PAIRS // 2)
+    def _(step):
+        pairs = [2 * step, 2 * step + 1]
+        g = lax.div(step, PAIRS // 2)
+        totals = [jnp.zeros((2 * SLOT, 2 * HEAD), F32) for _ in pairs]
         for column in range(5):
-            tile = scores[pair, :, column * TILE : (column + 1) * TILE]
-            weights = jnp.exp2((tile - top) * SCALE).astype(BF16)
             values = kv[g, column, 1] if column < 4 else own[g, 1]
-            total += jnp.dot(weights, jnp.concatenate([values, ones], 1), preferred_element_type=F32)
-        result = total[:, :HEAD] / total[:, HEAD:]
-        result = jnp.where(position[:, :HEAD] < length, result, 0.0).astype(BF16)
-        columns = pl.ds(pl.multiple_of(pair * 2 * HEAD, 2 * HEAD), 2 * HEAD)
-        out[:, columns] = jnp.concatenate([result[:SLOT], result[SLOT:]], 1)
-        pltpu.make_async_copy(out.at[:, columns], out_hbm.at[:, columns], local.at[5]).start()
+            values = jnp.concatenate([values, ones], 1)
+            for i, pair in enumerate(pairs):
+                top = jnp.concatenate([tops[pair], tops[pair]], 1)
+                tile = scores[pair, :, column * TILE : (column + 1) * TILE]
+                weights = jnp.exp2((tile - top) * SCALE).astype(BF16)
+                totals[i] += jnp.dot(weights, values, preferred_element_type=F32)
+        for pair, total in zip(pairs, totals):
+            result = total[:, :HEAD] / total[:, HEAD:]
+            result = jnp.where(position[:, :HEAD] < length, result, 0.0).astype(BF16)
+            columns = pl.ds(pl.multiple_of(pair * 2 * HEAD, 2 * HEAD), 2 * HEAD)
+            out[:, columns] = jnp.concatenate([result[:SLOT], result[SLOT:]], 1)
+            pltpu.make_async_copy(out.at[:, columns], out_hbm.at[:, columns], local.at[5]).start()
 
     keep.wait()
     keep_later.wait()
@@ -237,25 +251,30 @@
     carry_over = pltpu.make_async_copy(done, out.at[0], local.at[0])
     carry_over.start()
     length = lengths[1]
-    count = lax.div(length + TOKENS - 1, TOKENS)
-    units = 2 * count
+    full = lax.div(length + TOKENS // 2 - 1, TOKENS)
+    half = full * TOKENS < length
     ones = jnp.ones((TILE, HEAD), BF16)
 
-    def locate(unit):
-        g = (unit >= count).astype(jnp.int32)
-        return g, pl.multiple_of((unit - g * count) * TOKENS, TOKENS)
-
-    def step(current, scores_now, following, scores_next):
+    def store(token, tokens):
+        rows = pl.ds(pl.multiple_of(token, tokens), tokens)
+        pltpu.make_async_copy(result_ref.at[rows], out.at[1, rows], local.at[1]).start()
+
+    def step(tokens, current, scores_now, following, scores_next):
+        rows = tokens * HEADS
+        position = lax.rem(lax.broadcasted_iota(jnp.int32, (rows, TILE), 0), tokens)
         if following is not None:
-            g, token = locate(following)
-            rows = pl.ds(token, TOKENS)
-            queries = jnp.concatenate([q[1, rows, head_columns(g, h)] for h in range(HEADS)], 0)
+            g, token = following
+            token = pl.multiple_of(token, tokens)
+            queries = jnp.concatenate(
+                [q[1, pl.ds(token, tokens), head_columns(g, h)] for h in range(HEADS)], 0
+            )
             part_top = None
         if current is not None:
-            g_now, token_now = locate(current)
-            top = tops[...]
+            g_now, token_now = current
+            token_now = pl.multiple_of(token_now, tokens)
+            top = tops[:rows]
             top = jnp.concatenate([top, top], 1)
-            total = jnp.zeros((ROWS, 2 * HEAD), F32)
+            total = jnp.zeros((rows, 2 * HEAD), F32)
         for k in range(5):
             keys = slice(k * TILE, (k + 1) * TILE)
             if following is not None:
@@ -264,47 +283,64 @@
                     queries, source, (((1,), (1,)), ((), ())), preferred_element_type=F32
                 )
                 if k == 4:
-                    position = token + lax.rem(lax.broadcasted_iota(jnp.int32, (ROWS, TILE), 0), TOKENS)
-                    key = lax.broadcasted_iota(jnp.int32, (ROWS, TILE), 1)
-                    part = jnp.where((key <= position) & (key < length), part, NEG)
-                scores_next[:, keys] = part
+                    key = lax.broadcasted_iota(jnp.int32, (rows, TILE), 1)
+                    part = jnp.where((key <= position + token) & (key < length), part, NEG)
+                scores_next[:rows, keys] = part
                 part = jnp.maximum(part[:, :HEAD], part[:, HEAD:])
                 part_top = part if part_top is None else jnp.maximum(part_top, part)
             if current is not None:
-                weights = jnp.exp2((scores_now[:, keys] - top) * SCALE).astype(BF16)
+                weights = jnp.exp2((scores_now[:rows, keys] - top) * SCALE).astype(BF16)
                 source = prompt[g_now, k, 1] if k < 4 else own[g_now, 1]
                 total += jnp.dot(
                     weights, jnp.concatenate([source, ones], 1), preferred_element_type=F32
                 )
         if following is not None:
-            tops[...] = jnp.broadcast_to(jnp.max(part_top, -1, keepdims=True), (ROWS, HEAD))
+            tops[:rows] = jnp.broadcast_to(jnp.max(part_top, -1, keepdims=True), (rows, HEAD))
         if current is not None:
             result = total[:, :HEAD] / total[:, HEAD:]
-            position = token_now + lax.rem(lax.broadcasted_iota(jnp.int32, (ROWS, HEAD), 0), TOKENS)
-            result = jnp.where(position < length, result, 0.0).astype(BF16)
+            result = jnp.where(position[:, :HEAD] + token_now < length, result, 0.0).astype(BF16)
             for h in range(HEADS):
-                result_ref[pl.ds(token_now, TOKENS), head_columns(g_now, h)] = result[
-                    h * TOKENS : (h + 1) * TOKENS
+                result_ref[pl.ds(token_now, tokens), head_columns(g_now, h)] = result[
+                    h * tokens : (h + 1) * tokens
                 ]
 
-    @pl.loop(count, SLOT // TOKENS)
+    covered = full + half.astype(jnp.int32)
+
+    @pl.loop(covered, SLOT // TOKENS)
     def _(i):
-        result_ref[pl.ds(pl.multiple_of(i * TOKENS, TOKENS), TOKENS), :] = jnp.zeros(
-            (TOKENS, GROUPS * HEADS * HEAD), BF16
-        )
-
-    step(None, None, 0, scores_a)
-
-    @pl.loop(0, count)
-    def _(pair):
-        unit = 2 * pair
-        step(unit, scores_a, unit + 1, scores_b)
-        step(unit + 1, scores_b, jnp.minimum(unit + 2, units - 1), scores_a)
-
-    store = pltpu.make_async_copy(result_ref, out.at[1], local.at[1])
-    store.start()
+        token = pl.multiple_of(i * TOKENS, TOKENS)
+        result_ref[pl.ds(token, TOKENS), :] = jnp.zeros((TOKENS, GROUPS * HEADS * HEAD), BF16)
+        store(token, TOKENS)
+
+    @pl.when(full > 0)
+    def _():
+        step(TOKENS, None, None, (0, 0), scores_a)
+
+        @pl.loop(0, full - 1)
+        def _(i):
+            token = i * TOKENS
+            step(TOKENS, (0, token), scores_a, (1, token), scores_b)
+            step(TOKENS, (1, token), scores_b, (0, token + TOKENS), scores_a)
+            store(token, TOKENS)
+
+        token = (full - 1) * TOKENS
+        step(TOKENS, (0, token), scores_a, (1, token), scores_b)
+        step(TOKENS, (1, token), scores_b, None, None)
+        store(token, TOKENS)
+
+    @pl.when(half)
+    def _():
+        tokens = TOKENS // 2
+        token = full * TOKENS
+        step(tokens, None, None, (0, token), scores_a)
+        step(tokens, (0, token), scores_a, (1, token), scores_b)
+        step(tokens, (1, token), scores_b, None, None)
+        rest = pl.ds(pl.multiple_of(token + tokens, tokens), tokens)
+        result_ref[rest, :] = jnp.zeros((tokens, GROUPS * HEADS * HEAD), BF16)
+        store(token, TOKENS)
+
+    pltpu.make_async_copy(result_ref, out.at[1], local.at[1]).wait()
     carry_over.wait()
-    store.wait()
 
 
 def second(lengths, queries, own, prompt, done):

time: 32.8 us -> 31.2 us (0.951)
  Pallas kernels: 32.7 us -> 31.1 us
    pallas_call x1, Pallas kernels: 7.26 us -> 6.25 us  [second(): pl.pallas_call(second_kernel, in_specs=[pl.BlockSpec(memory_space=pltpu.S...]
    pallas_call x1, Pallas kernels: 25.4 us -> 24.9 us  [first(): pl.pallas_call(first_kernel, in_specs=[pl.BlockSpec(memory_space=pltpu.HB...]
where the time goes in v3:
time: 31.2 us; the launch traced here: 31.1 us
  Pallas kernels  31.1 us (100%)
    pallas_call x1, Pallas kernels, first(): pl.pallas_call(first_kernel, in_specs=[pl.BlockSpec(memory_space=pltpu.HB...  24.9 us
    pallas_call x1, Pallas kernels, second(): pl.pallas_call(second_kernel, in_specs=[pl.BlockSpec(memory_space=pltpu.S...  6.25 us

profile of v3, /device:TPU:1, one launch (start us, length us, event | category | flops | bytes accessed | tf_op | source)
XLA Modules:
  0.0 31.1 jit_solution(12508071888839113774)
XLA Ops:
  0.0 0.0 copy-start.1
  0.0 0.0 copy-start
  0.0 24.9 %shard_map.46 = (bf16[256,2048]{1,0:T(8,128)(2,1)S(1)}, bf16[2,4,2,256,128]{4,3,2,1,0:T(8,128)(2,1)S(1)}, bf16[2,2,256,128]{3,2,1,0:T(8,128)(2,1)S(1)}) custom-call(s32[2]{0:T(128)} %bitcast.8, bf16[8,2,512]{2,1,0:T(2,128)(2,1)} %shard_hbm.1, bf16[2,256,2048]{2,1,0:T(8,128)(2,1)} %bitcast.6, bf16[2,256,2,256]{3,2,1,0:T(2,128)(2,1)} %bitcast.10), custom_call_target="tpu_custom_call" | custom-call | tf_op jit(solution)/shard_map/pallas_call | solution.py:220
  24.9 0.0 copy-done.1
  24.9 0.0 copy-done
  24.9 6.3 %shard_map.47 = bf16[2,256,2048]{2,1,0:T(8,128)(2,1)} custom-call(s32[2]{0:T(128)S(1)} %bitcast.9, bf16[2,256,2048]{2,1,0:T(8,128)(2,1)S(1)} %bitcast.7, bf16[2,2,256,128]{3,2,1,0:T(8,128)(2,1)S(1)} %get-tuple-element.8.own, bf16[2,4,2,256,128]{4,3,2,1,0:T(8,128)(2,1)S(1)} %get-tuple-element.9.prompt, bf16[256,2048]{1,0:T(8,128)(2,1)S(1)} %get-tuple-element.10.done), custom_call_target="tpu_custom_call" | custom-call | tf_op jit(solution)/shard_map/pallas_call | solution.py:348
Async XLA Ops:
  0.0 24.9 %copy-start.1 = (s32[2,1]{0,1:T(1,128)S(1)}, s32[2,1]{0,1:T(1,128)}, u32[]{:S(2)}) copy-start(s32[2,1]{0,1:T(1,128)} %param.6) | copy-start | bytes 28
  0.0 24.9 %copy-start = (bf16[2,1,256,2048]{3,2,1,0:T(8,128)(2,1)S(1)}, bf16[2,1,256,2048]{3,2,1,0:T(8,128)(2,1)}, u32[]{:S(2)}) copy-start(bf16[2,1,256,2048]{3,2,1,0:T(8,128)(2,1)} %param.4) | copy-start | bytes 6291460

commit v4 on v3

--- a/solution.py
+++ b/solution.py
@@ -61,7 +61,7 @@
 
 def first_kernel(
     lengths_hbm, shard_hbm, queries, trace_kv, out_hbm, kv_out, later_out,
-    lengths, blocks, kv, shard, stage, q, raw, own, later, out, scores, tops,
+    lengths, blocks, kv, shard, stage, q, raw, own, later, out, scores, tops, partial,
     s1, r1, s3, r3, local,
 ):
     x, y, z, core = coordinates()
@@ -106,17 +106,19 @@
     for k in range(2):
         blocks[core, k, here] = stage[tensor, k]
 
-    def scores_of(g, column, keys, mask=None):
+    def scores_of(g, columns, mask=None):
         for j in range(PAIRS):
             pair = jnp.concatenate([q[:, head_columns(g, 2 * j)], q[:, head_columns(g, 2 * j + 1)]], 0)
-            tile = lax.dot_general(pair, keys, (((1,), (1,)), ((), ())), preferred_element_type=F32)
-            if mask is not None:
-                tile = jnp.where(mask, tile, NEG)
-            scores[g * PAIRS + j, :, column * TILE : (column + 1) * TILE] = tile
-            tile = jnp.maximum(tile[:, :HEAD], tile[:, HEAD:])
-            if mask is None:
-                tile = jnp.maximum(tops[g * PAIRS + j], tile)
-            tops[g * PAIRS + j] = tile
+            top = None if mask is not None else tops[g * PAIRS + j]
+            for column in columns:
+                keys = kv[g, column, 0] if column < 4 else own[g, 0]
+                tile = lax.dot_general(pair, keys, (((1,), (1,)), ((), ())), preferred_element_type=F32)
+                if mask is not None:
+                    tile = jnp.where(mask, tile, NEG)
+                scores[g * PAIRS + j, :, column * TILE : (column + 1) * TILE] = tile
+                tile = jnp.maximum(tile[:, :HEAD], tile[:, HEAD:])
+                top = tile if top is None else jnp.maximum(top, tile)
+            tops[g * PAIRS + j] = top
 
     load_own.wait()
     for s, target in ((0, own), (1, later)):
@@ -134,7 +136,7 @@
 
     @pl.loop(0, GROUPS)
     def _(g):
-        scores_of(g, 4, own[g, 0], allowed)
+        scores_of(g, (4,), allowed)
 
     def group(side, k, d):
         return blocks.at[side, k, pl.ds(pl.multiple_of(turn(x, d) * 16, 16), 16)]
@@ -158,50 +160,59 @@
             landed(group(1 - core, k, d), r3.at[k, d])
         arrange(1 - core, column, k)
 
-    def prompt_scores(column):
-        @pl.loop(0, GROUPS)
-        def _(g):
-            scores_of(g, column, kv[g, column, 0])
-
     for column in (0, 1):
         collect(0, column)
-    for column in (0, 1):
-        prompt_scores(column)
-    collect_partner(0, 2)
-    prompt_scores(2)
-    for column in (0, 1):
-        collect(1, column)
-    collect_partner(0, 3)
+
+    @pl.loop(0, GROUPS)
+    def _(g):
+        scores_of(g, (0, 1))
+
+    for column in (2, 3):
+        collect_partner(0, column)
     for g in range(GROUPS):
-        scores_of(g, 3, kv[g, 3, 0])
+        scores_of(g, (2, 3))
         for pair in range(g * PAIRS, (g + 1) * PAIRS):
             tops[pair] = jnp.broadcast_to(jnp.max(tops[pair], -1, keepdims=True), (2 * SLOT, HEAD))
-    for column in (2, 3):
-        collect_partner(1, column)
-    keep = pltpu.make_async_copy(kv, kv_out, local.at[2])
-    keep.start()
-
+        if g == 0:
+            collect(1, 0)
+            collect(1, 1)
     ones = jnp.ones((TILE, HEAD), BF16)
 
-    @pl.loop(0, GROUPS * PAIRS // 2)
-    def _(step):
-        pairs = [2 * step, 2 * step + 1]
+    def attended(step, columns):
         g = lax.div(step, PAIRS // 2)
-        totals = [jnp.zeros((2 * SLOT, 2 * HEAD), F32) for _ in pairs]
-        for column in range(5):
+        totals = [None, None]
+        for column in columns:
             values = kv[g, column, 1] if column < 4 else own[g, 1]
             values = jnp.concatenate([values, ones], 1)
-            for i, pair in enumerate(pairs):
+            for i in range(2):
+                pair = 2 * step + i
                 top = jnp.concatenate([tops[pair], tops[pair]], 1)
                 tile = scores[pair, :, column * TILE : (column + 1) * TILE]
                 weights = jnp.exp2((tile - top) * SCALE).astype(BF16)
-                totals[i] += jnp.dot(weights, values, preferred_element_type=F32)
-        for pair, total in zip(pairs, totals):
+                total = jnp.dot(weights, values, preferred_element_type=F32)
+                totals[i] = total if totals[i] is None else totals[i] + total
+        return totals
+
+    def finish(step, totals):
+        for i, total in enumerate(totals):
+            pair = 2 * step + i
             result = total[:, :HEAD] / total[:, HEAD:]
             result = jnp.where(position[:, :HEAD] < length, result, 0.0).astype(BF16)
             columns = pl.ds(pl.multiple_of(pair * 2 * HEAD, 2 * HEAD), 2 * HEAD)
             out[:, columns] = jnp.concatenate([result[:SLOT], result[SLOT:]], 1)
             pltpu.make_async_copy(out.at[:, columns], out_hbm.at[:, columns], local.at[5]).start()
+
+    for i, total in enumerate(attended(0, (4, 0, 1))):
+        partial[i] = total
+    for column in (2, 3):
+        collect_partner(1, column)
+    keep = pltpu.make_async_copy(kv, kv_out, local.at[2])
+    keep.start()
+    finish(0, [partial[i] + total for i, total in enumerate(attended(0, (2, 3)))])
+
+    @pl.loop(1, PAIRS)
+    def _(step):
+        finish(step, attended(step, (0, 1, 2, 3, 4)))
 
     keep.wait()
     keep_later.wait()
@@ -239,6 +250,7 @@
             vmem((SLOT, columns), BF16),
             vmem((2 * PAIRS, 2 * SLOT, PROMPT + SLOT), F32),
             vmem((2 * PAIRS, 2 * SLOT, HEAD), F32),
+            vmem((2, 2 * SLOT, 2 * HEAD), F32),
             dma((2,)), dma((2, 4)), dma((2, 4)), dma((2, 4)), dma((7,)),
         ],
         compiler_params=pltpu.CompilerParams(

time: 31.2 us -> 30.3 us (0.971)
  Pallas kernels: 31.1 us -> 30.2 us
    pallas_call x1, Pallas kernels: 24.9 us -> 24 us  [first(): pl.pallas_call(first_kernel, in_specs=[pl.BlockSpec(memory_space=pltpu.HB...]
where the time goes in v4:
time: 30.3 us; the launch traced here: 30.2 us
  Pallas kernels  30.2 us (100%)
    pallas_call x1, Pallas kernels, first(): pl.pallas_call(first_kernel, in_specs=[pl.BlockSpec(memory_space=pltpu.HB...  24 us
    pallas_call x1, Pallas kernels, second(): pl.pallas_call(second_kernel, in_specs=[pl.BlockSpec(memory_space=pltpu.S...  6.25 us

profile of v4, /device:TPU:1, one launch (start us, length us, event | category | flops | bytes accessed | tf_op | source)
XLA Modules:
  0.0 30.2 jit_solution(12267016639400787774)
XLA Ops:
  0.0 0.0 copy-start.1
  0.0 0.0 copy-start
  0.0 24.0 %shard_map.46 = (bf16[256,2048]{1,0:T(8,128)(2,1)S(1)}, bf16[2,4,2,256,128]{4,3,2,1,0:T(8,128)(2,1)S(1)}, bf16[2,2,256,128]{3,2,1,0:T(8,128)(2,1)S(1)}) custom-call(s32[2]{0:T(128)} %bitcast.8, bf16[8,2,512]{2,1,0:T(2,128)(2,1)} %shard_hbm.1, bf16[2,256,2048]{2,1,0:T(8,128)(2,1)} %bitcast.6, bf16[2,256,2,256]{3,2,1,0:T(2,128)(2,1)} %bitcast.10), custom_call_target="tpu_custom_call" | custom-call | tf_op jit(solution)/shard_map/pallas_call | solution.py:231
  24.0 0.0 copy-done.1
  24.0 0.0 copy-done
  24.0 6.3 %shard_map.47 = bf16[2,256,2048]{2,1,0:T(8,128)(2,1)} custom-call(s32[2]{0:T(128)S(1)} %bitcast.9, bf16[2,256,2048]{2,1,0:T(8,128)(2,1)S(1)} %bitcast.7, bf16[2,2,256,128]{3,2,1,0:T(8,128)(2,1)S(1)} %get-tuple-element.8.own, bf16[2,4,2,256,128]{4,3,2,1,0:T(8,128)(2,1)S(1)} %get-tuple-element.9.prompt, bf16[256,2048]{1,0:T(8,128)(2,1)S(1)} %get-tuple-element.10.done), custom_call_target="tpu_custom_call" | custom-call | tf_op jit(solution)/shard_map/pallas_call | solution.py:360
Async XLA Ops:
  0.0 24.0 %copy-start.1 = (s32[2,1]{0,1:T(1,128)S(1)}, s32[2,1]{0,1:T(1,128)}, u32[]{:S(2)}) copy-start(s32[2,1]{0,1:T(1,128)} %param.6) | copy-start | bytes 28
  0.0 24.0 %copy-start = (bf16[2,1,256,2048]{3,2,1,0:T(8,128)(2,1)S(1)}, bf16[2,1,256,2048]{3,2,1,0:T(8,128)(2,1)}, u32[]{:S(2)}) copy-start(bf16[2,1,256,2048]{3,2,1,0:T(8,128)(2,1)} %param.4) | copy-start | bytes 6291460

commit v5 on v4

--- a/solution.py
+++ b/solution.py
@@ -194,13 +194,14 @@
         return totals
 
     def finish(step, totals):
-        for i, total in enumerate(totals):
-            pair = 2 * step + i
+        results = []
+        for total in totals:
             result = total[:, :HEAD] / total[:, HEAD:]
             result = jnp.where(position[:, :HEAD] < length, result, 0.0).astype(BF16)
-            columns = pl.ds(pl.multiple_of(pair * 2 * HEAD, 2 * HEAD), 2 * HEAD)
-            out[:, columns] = jnp.concatenate([result[:SLOT], result[SLOT:]], 1)
-            pltpu.make_async_copy(out.at[:, columns], out_hbm.at[:, columns], local.at[5]).start()
+            results += [result[:SLOT], result[SLOT:]]
+        columns = pl.ds(pl.multiple_of(step * 4 * HEAD, 4 * HEAD), 4 * HEAD)
+        out[:, columns] = jnp.concatenate(results, 1)
+        pltpu.make_async_copy(out.at[:, columns], out_hbm.at[:, columns], local.at[5]).start()
 
     for i, total in enumerate(attended(0, (4, 0, 1))):
         partial[i] = total

time: 30.3 us -> 30 us (0.990)
  no operation moved by 1% of the time
where the time goes in v5:
time: 30 us; the launch traced here: 29.9 us
  Pallas kernels  29.9 us (100%)
    pallas_call x1, Pallas kernels, first(): pl.pallas_call(first_kernel, in_specs=[pl.BlockSpec(memory_space=pltpu.HB...  23.6 us
    pallas_call x1, Pallas kernels, second(): pl.pallas_call(second_kernel, in_specs=[pl.BlockSpec(memory_space=pltpu.S...  6.25 us

profile of v5, /device:TPU:1, one launch (start us, length us, event | category | flops | bytes accessed | tf_op | source)
XLA Modules:
  0.0 29.9 jit_solution(810569562713914163)
XLA Ops:
  0.0 0.0 copy-start.1
  0.0 0.0 copy-start
  0.0 23.6 %shard_map.46 = (bf16[256,2048]{1,0:T(8,128)(2,1)S(1)}, bf16[2,4,2,256,128]{4,3,2,1,0:T(8,128)(2,1)S(1)}, bf16[2,2,256,128]{3,2,1,0:T(8,128)(2,1)S(1)}) custom-call(s32[2]{0:T(128)} %bitcast.8, bf16[8,2,512]{2,1,0:T(2,128)(2,1)} %shard_hbm.1, bf16[2,256,2048]{2,1,0:T(8,128)(2,1)} %bitcast.6, bf16[2,256,2,256]{3,2,1,0:T(2,128)(2,1)} %bitcast.10), custom_call_target="tpu_custom_call" | custom-call | tf_op jit(solution)/shard_map/pallas_call | solution.py:232
  23.7 0.0 copy-done.1
  23.7 0.0 copy-done
  23.7 6.3 %shard_map.47 = bf16[2,256,2048]{2,1,0:T(8,128)(2,1)} custom-call(s32[2]{0:T(128)S(1)} %bitcast.9, bf16[2,256,2048]{2,1,0:T(8,128)(2,1)S(1)} %bitcast.7, bf16[2,2,256,128]{3,2,1,0:T(8,128)(2,1)S(1)} %get-tuple-element.8.own, bf16[2,4,2,256,128]{4,3,2,1,0:T(8,128)(2,1)S(1)} %get-tuple-element.9.prompt, bf16[256,2048]{1,0:T(8,128)(2,1)S(1)} %get-tuple-element.10.done), custom_call_target="tpu_custom_call" | custom-call | tf_op jit(solution)/shard_map/pallas_call | solution.py:361
Async XLA Ops:
  0.0 23.7 %copy-start.1 = (s32[2,1]{0,1:T(1,128)S(1)}, s32[2,1]{0,1:T(1,128)}, u32[]{:S(2)}) copy-start(s32[2,1]{0,1:T(1,128)} %param.6) | copy-start | bytes 28
  0.0 23.7 %copy-start = (bf16[2,1,256,2048]{3,2,1,0:T(8,128)(2,1)S(1)}, bf16[2,1,256,2048]{3,2,1,0:T(8,128)(2,1)}, u32[]{:S(2)}) copy-start(bf16[2,1,256,2048]{3,2,1,0:T(8,128)(2,1)} %param.4) | copy-start | bytes 6291460

commit v6 on v5

--- a/solution.py
+++ b/solution.py
@@ -163,8 +163,7 @@
     for column in (0, 1):
         collect(0, column)
 
-    @pl.loop(0, GROUPS)
-    def _(g):
+    for g in range(GROUPS):
         scores_of(g, (0, 1))
 
     for column in (2, 3):

time: 30 us -> 29.9 us (level)
  no operation moved by 1% of the time
where the time goes in v6:
time: 29.9 us; the launch traced here: 29.7 us
  Pallas kernels  29.7 us (99%)
    pallas_call x1, Pallas kernels, first(): pl.pallas_call(first_kernel, in_specs=[pl.BlockSpec(memory_space=pltpu.HB...  23.5 us
    pallas_call x1, Pallas kernels, second(): pl.pallas_call(second_kernel, in_specs=[pl.BlockSpec(memory_space=pltpu.S...  6.25 us

profile of v6, /device:TPU:1, one launch (start us, length us, event | category | flops | bytes accessed | tf_op | source)
XLA Modules:
  0.0 29.7 jit_solution(13445217826702971673)
XLA Ops:
  0.0 0.0 copy-start.1
  0.0 0.0 copy-start
  0.0 23.5 %shard_map.46 = (bf16[256,2048]{1,0:T(8,128)(2,1)S(1)}, bf16[2,4,2,256,128]{4,3,2,1,0:T(8,128)(2,1)S(1)}, bf16[2,2,256,128]{3,2,1,0:T(8,128)(2,1)S(1)}) custom-call(s32[2]{0:T(128)} %bitcast.8, bf16[8,2,512]{2,1,0:T(2,128)(2,1)} %shard_hbm.1, bf16[2,256,2048]{2,1,0:T(8,128)(2,1)} %bitcast.6, bf16[2,256,2,256]{3,2,1,0:T(2,128)(2,1)} %bitcast.10), custom_call_target="tpu_custom_call" | custom-call | tf_op jit(solution)/shard_map/pallas_call | solution.py:231
  23.5 0.0 copy-done.1
  23.5 0.0 copy-done
  23.5 6.3 %shard_map.47 = bf16[2,256,2048]{2,1,0:T(8,128)(2,1)} custom-call(s32[2]{0:T(128)S(1)} %bitcast.9, bf16[2,256,2048]{2,1,0:T(8,128)(2,1)S(1)} %bitcast.7, bf16[2,2,256,128]{3,2,1,0:T(8,128)(2,1)S(1)} %get-tuple-element.8.own, bf16[2,4,2,256,128]{4,3,2,1,0:T(8,128)(2,1)S(1)} %get-tuple-element.9.prompt, bf16[256,2048]{1,0:T(8,128)(2,1)S(1)} %get-tuple-element.10.done), custom_call_target="tpu_custom_call" | custom-call | tf_op jit(solution)/shard_map/pallas_call | solution.py:360
Async XLA Ops:
  0.0 23.5 %copy-start.1 = (s32[2,1]{0,1:T(1,128)S(1)}, s32[2,1]{0,1:T(1,128)}, u32[]{:S(2)}) copy-start(s32[2,1]{0,1:T(1,128)} %param.6) | copy-start | bytes 28
  0.0 23.5 %copy-start = (bf16[2,1,256,2048]{3,2,1,0:T(8,128)(2,1)S(1)}, bf16[2,1,256,2048]{3,2,1,0:T(8,128)(2,1)}, u32[]{:S(2)}) copy-start(bf16[2,1,256,2048]{3,2,1,0:T(8,128)(2,1)} %param.4) | copy-start | bytes 6291460
